TPU v7x, 32 devices: a whole 2x2x4 slice. The times are simulated.
32 devices in a mesh: sector: 4 (over y, core), term: 8 (over z, x).
Axes of the slice: x: 2, y: 2, z: 4, core: 2. Of those that a mesh axis runs over, the one named last changes fastest.
Arguments:
- trial: float32 [8, 512, 512], P('sector', 'term'), may hold values from -6 to 6
- precond: float32 [8, 512, 512], P('sector', 'term'), may hold values from 2 to 16
- sector_dims: int32 [8], P('sector'), may hold values from 128 to 512
- left_ops: float32 [256, 512, 512], P(('sector', 'term')), may hold values from -0.25 to 0.25
- right_ops: float32 [256, 512, 512], P(('sector', 'term')), may hold values from -0.25 to 0.25
- task_source: int32 [256], P(('sector', 'term')), may hold values from 0 to 1
- task_target: int32 [256], P(('sector', 'term')), may hold values from 0 to 1
- task_count: int32 [32], P(('sector', 'term')), may hold values from 1 to 7, as said below
Outputs:
- trial_out: float32 [8, 512, 512], P('sector', 'term')
- ritz: float32 [3], replicated
Inputs may be any that keep to these rules, and one draw needn't show every extreme that they name: `task_count`: the counts of two devices with the same sector index whose term indices differ by half the term axis add up to 8.
All inputs are finite; a program needn't handle non-finite values.
Results may differ from a plain program's by a relative error of at most 0.0003.
Values sent between devices are 32-bit elements; how exact they have to be, the bound alone decides.
No kernel may reach another device: no remote copies, remote signals or barrier semaphores. Data moves between devices by JAX's collectives and lax.ppermute only.
A program may use at most 64 MiB of HBM per device.

v0:
```python
import jax
import jax.numpy as jnp
from jax import lax
from jax.sharding import PartitionSpec as P

STEPS = 3


def apply_tasks(partial_value, full_vector, lefts, rights, sources, targets, first, last):
    highest = lax.Precision.HIGHEST

    def one(slot, total):
        block = lax.dynamic_index_in_dim(full_vector, sources[slot], 0, keepdims=False)
        inner = jnp.dot(block, rights[slot], precision=highest)
        product = jnp.dot(lefts[slot], inner, precision=highest)
        old = lax.dynamic_index_in_dim(total, targets[slot], 0, keepdims=True)
        return lax.dynamic_update_index_in_dim(total, old + product[None], targets[slot], 0)

    return lax.fori_loop(first, last, one, partial_value)


def rescale(vector, cells):
    total = lax.psum(jnp.sum(vector * vector), ("sector", "term"))
    return vector * jnp.sqrt(cells / total)


def per_device(
    trial, precond, sector_dims, left_ops, right_ops, task_source, task_target, task_count
):
    sec_dev, share, width = trial.shape
    cells = float(sec_dev * lax.axis_size("sector") * width * width)
    start = lax.axis_index("term") * share
    rows = start + jnp.arange(share, dtype=jnp.int32)
    cols = jnp.arange(width, dtype=jnp.int32)
    limits = sector_dims[:, None]
    mask = ((rows[None, :] < limits)[:, :, None] & (cols[None, :] < limits)[:, None, :]).astype(
        jnp.float32
    )
    count = task_count[0]
    values = []
    vector = mask * trial
    for step in range(STEPS):
        full_vector = lax.all_gather(vector, "term", axis=1, tiled=True)
        partial_value = jnp.zeros((sec_dev, width, width), jnp.float32)
        partial_value = apply_tasks(
            partial_value, full_vector, left_ops, right_ops, task_source, task_target, 0, count
        )
        whole = lax.psum(partial_value, "term")
        summed = lax.dynamic_slice_in_dim(whole, start, share, 1)
        sig = summed * mask
        sums = lax.psum((jnp.sum(vector * sig), jnp.sum(vector * vector)), ("sector", "term"))
        theta = sums[0] / sums[1]
        values.append(theta)
        vector = vector - (sig - theta * vector) / precond
    vector = rescale(vector, cells)
    return (vector, jnp.stack(values))


def solution(mesh):
    return jax.shard_map(
        per_device,
        mesh=mesh,
        in_specs=(
            P("sector", "term", None),
            P("sector", "term", None),
            P("sector"),
            P(("sector", "term"), None, None),
            P(("sector", "term"), None, None),
            P(("sector", "term")),
            P(("sector", "term")),
            P(("sector", "term")),
        ),
        out_specs=(P("sector", "term", None), P()),
        check_vma=False,
    )
```

profile of v0, /device:TPU:0, one launch (start us, length us, event | category | flops | bytes accessed | tf_op | source)
XLA Modules:
  0.0 907.3 jit_solution(15837451852060297039)
XLA Ops:
  10.5 52.2 %all-gather.4.cloned.1.call-done = f32[2,512,512]{2,1,0:T(8,128)} async-done(((f32[2,64,512]{2,1,0:T(8,128)}), f32[2,512,512]{2,1,0:T(8,128)}) %all-gather.4.cloned.1.call-update) | async-done | bytes 2097168 | tf_op jit(solution)/shard_map/all_gather | solution.py:43
  63.0 86.0 %while.30 = (s32[]{:T(128)}, f32[2,512,512]{2,1,0:T(8,128)S(1)}, s32[]{:T(128)}, s32[8]{0:T(128)S(1)}, f32[8,512,512]{2,1,0:T(8,128)}, /*index=5*/s32[8]{0:T(128...) while((s32[]{:T(128)}, f32[2,512,512]{2,1,0:T(8,128)S(1)}, ...), condition=%wide.region_1.2_spmd, body=%wide.region_0.1_spmd.sunk | while | flops 3221487616 | bytes 7340291 | solution.py:19
  66.2 3.4 fusion.58
  78.4 3.4 fusion.58
  90.6 3.4 fusion.58
  102.8 3.4 fusion.58
  115.0 3.4 fusion.58
  139.4 3.4 fusion.58
  150.5 100.4 %all-reduce.7.cloned.1.call-done = f32[2,512,512]{2,1,0:T(8,128)} async-done(((f32[2,512,512]{2,1,0:T(8,128)}), f32[2,512,512]{2,1,0:T(8,128)}) %all-reduce.7.cloned.1.call-update) | async-done | bytes 2097168 | tf_op jit(solution)/shard_map/psum | solution.py:48
  252.5 40.4 %all-reduce.2 = (f32[]{:T(128)}, f32[]{:T(128)}) all-reduce(f32[]{:T(128)} %get-tuple-element.139, f32[]{:T(128)} %get-tuple-element.138), channel_id=1, replica_groups=mesh['sector'=4,'term'=8] {'sector','term'}, use_global_device_ids=true, to_apply=%region_4.5 | all-reduce | flops 2 | bytes 16 | tf_op jit(solution)/shard_map/psum | solution.py:51
  296.1 49.1 %all-gather.6.cloned.1.call-done = f32[2,512,512]{2,1,0:T(8,128)} async-done(((f32[2,64,512]{2,1,0:T(8,128)}), f32[2,512,512]{2,1,0:T(8,128)}) %all-gather.6.cloned.1.call-update) | async-done | bytes 2097168 | tf_op jit(solution)/shard_map/all_gather | solution.py:43
  345.6 84.9 %while.31 = (s32[]{:T(128)}, f32[2,512,512]{2,1,0:T(8,128)S(1)}, s32[]{:T(128)}, s32[8]{0:T(128)S(1)}, f32[8,512,512]{2,1,0:T(8,128)}, /*index=5*/s32[8]{0:T(128...) while((s32[]{:T(128)}, f32[2,512,512]{2,1,0:T(8,128)S(1)}, ...), condition=%wide.region_8.9_spmd, body=%wide.region_7.8_spmd.sunk | while | flops 3221487616 | bytes 7340291 | solution.py:19
  348.7 3.4 fusion.64
  360.7 3.4 fusion.64
  431.8 100.3 %all-reduce.9.cloned.1.call-done = f32[2,512,512]{2,1,0:T(8,128)} async-done(((f32[2,512,512]{2,1,0:T(8,128)}), f32[2,512,512]{2,1,0:T(8,128)}) %all-reduce.9.cloned.1.call-update) | async-done | bytes 2097168 | tf_op jit(solution)/shard_map/psum | solution.py:48
  533.9 40.4 %all-reduce.1 = (f32[]{:T(128)}, f32[]{:T(128)}) all-reduce(f32[]{:T(128)} %get-tuple-element.137, f32[]{:T(128)} %get-tuple-element.136), channel_id=1, replica_groups=mesh['sector'=4,'term'=8] {'sector','term'}, use_global_device_ids=true, to_apply=%region_11.12 | all-reduce | flops 2 | bytes 16 | tf_op jit(solution)/shard_map/psum | solution.py:51
  577.5 49.1 %all-gather.8.cloned.1.call-done = f32[2,512,512]{2,1,0:T(8,128)} async-done(((f32[2,64,512]{2,1,0:T(8,128)}), f32[2,512,512]{2,1,0:T(8,128)}) %all-gather.8.cloned.1.call-update) | async-done | bytes 2097168 | tf_op jit(solution)/shard_map/all_gather | solution.py:43
  626.9 85.1 %while.32 = (s32[]{:T(128)}, f32[2,512,512]{2,1,0:T(8,128)S(1)}, s32[]{:T(128)}, s32[8]{0:T(128)S(1)}, f32[8,512,512]{2,1,0:T(8,128)}, /*index=5*/s32[8]{0:T(128...) while((s32[]{:T(128)}, f32[2,512,512]{2,1,0:T(8,128)S(1)}, ...), condition=%wide.region_15.16_spmd, body=%wide.region_14.15_spmd.sunk | while | flops 3221487616 | bytes 7340291 | solution.py:19
  630.2 3.4 fusion.70
  654.2 3.4 fusion.70
  678.3 3.4 fusion.70
  713.3 100.5 %all-reduce.11.cloned.1.call-done = f32[2,512,512]{2,1,0:T(8,128)} async-done(((f32[2,512,512]{2,1,0:T(8,128)}), f32[2,512,512]{2,1,0:T(8,128)}) %all-reduce.11.cloned.1.call-update) | async-done | bytes 2097168 | tf_op jit(solution)/shard_map/psum | solution.py:48
  815.5 40.4 %all-reduce = (f32[]{:T(128)}, f32[]{:T(128)}) all-reduce(f32[]{:T(128)} %get-tuple-element.135, f32[]{:T(128)} %get-tuple-element.134), channel_id=1, replica_groups=mesh['sector'=4,'term'=8] {'sector','term'}, use_global_device_ids=true, to_apply=%region_18.19 | all-reduce | flops 2 | bytes 16 | tf_op jit(solution)/shard_map/psum | solution.py:51
  858.9 39.4 %psum.79 = f32[]{:T(128)} all-reduce(f32[]{:T(128)} %get-tuple-element.194), channel_id=1, replica_groups=mesh['sector'=4,'term'=8] {'sector','term'}, use_global_device_ids=true, to_apply=%region_22.23 | all-reduce | flops 1 | bytes 8 | tf_op jit(solution)/shard_map/psum | solution.py:23
  (118 shorter events, 143.1 us)
Async XLA Ops:
  7.2 55.9 %copy-start.8 = (s32[8]{0:T(128)S(1)}, s32[8]{0:T(128)}, u32[]{:S(2)}) copy-start(s32[8]{0:T(128)} %param.19) | copy-start | bytes 100
  7.2 55.9 %copy-start.7 = (s32[8]{0:T(128)S(1)}, s32[8]{0:T(128)}, u32[]{:S(2)}) copy-start(s32[8]{0:T(128)} %param.20) | copy-start | bytes 100
  7.2 55.6 %all-gather.4.cloned.1.call-start = ((), (), s32[]{:S(2)}) async-start(), calls=%async_computation | async-start | bytes 2359296 | tf_op jit(solution)/shard_map/all_gather | solution.py:43
  10.5 240.4 %all-reduce.7.cloned.1.call-start = ((), (), s32[]{:S(2)}) async-start(), calls=%async_computation.1 | async-start | bytes 4194304 | tf_op jit(solution)/shard_map/psum | solution.py:48
  149.1 1.3 copy-start.1
  149.1 101.7 %copy-start.5 = (f32[2,64,512]{2,1,0:T(8,128)S(1)}, f32[2,64,512]{2,1,0:T(8,128)}, u32[]{:S(2)}) copy-start(f32[2,64,512]{2,1,0:T(8,128)} %param.14) | copy-start | bytes 786436
  149.1 145.1 %copy-start.6 = (f32[2,64,512]{2,1,0:T(8,128)S(1)}, f32[2,64,512]{2,1,0:T(8,128)}, u32[]{:S(2)}) copy-start(f32[2,64,512]{2,1,0:T(8,128)} %param.15) | copy-start | bytes 786436
  150.4 194.9 %all-gather.6.cloned.1.call-start = ((), (), s32[]{:S(2)}) async-start(), calls=%async_computation.2 | async-start | bytes 2359296 | tf_op jit(solution)/shard_map/all_gather | solution.py:43
  296.1 236.1 %all-reduce.9.cloned.1.call-start = ((), (), s32[]{:S(2)}) async-start(), calls=%async_computation.3 | async-start | bytes 4194304 | tf_op jit(solution)/shard_map/psum | solution.py:48
  430.5 1.3 copy-start.2
  430.5 101.7 %copy-start.3 = (f32[2,64,512]{2,1,0:T(8,128)S(1)}, f32[2,64,512]{2,1,0:T(8,128)}, u32[]{:S(2)}) copy-start(f32[2,64,512]{2,1,0:T(8,128)} %divide_subtract_fusion.2) | copy-start | bytes 786436
  431.8 194.8 %all-gather.8.cloned.1.call-start = ((), (), s32[]{:S(2)}) async-start(), calls=%async_computation.4 | async-start | bytes 2359296 | tf_op jit(solution)/shard_map/all_gather | solution.py:43
  577.4 236.3 %all-reduce.11.cloned.1.call-start = ((), (), s32[]{:S(2)}) async-start(), calls=%async_computation.5 | async-start | bytes 4194304 | tf_op jit(solution)/shard_map/psum | solution.py:48
  711.9 1.3 copy-start
  712.0 101.8 %copy-start.4 = (f32[2,64,512]{2,1,0:T(8,128)S(1)}, f32[2,64,512]{2,1,0:T(8,128)}, u32[]{:S(2)}) copy-start(f32[2,64,512]{2,1,0:T(8,128)} %divide_subtract_fusion.1) | copy-start | bytes 786436
Sparse Core Ops, SparseCore 0:
  10.8 51.9 all-gather.3
  150.5 100.2 all-reduce.6
  296.2 49.0 all-gather.5
  431.9 100.2 all-reduce.8
  577.5 49.0 all-gather.7
  713.4 100.3 all-reduce.10
where the time goes:
time: 911 us; the launch traced here: 907 us
  waiting for transfers between devices  452 us (50%)
  blocking collectives  161 us (18%)
  matrix products  135 us (15%)
  loops' own time  95.6 us (10%)
  local copies, waits for them, and re-layouts  29.5 us (3%)
  between operations  19 us (2%)
  other arithmetic  15 us (2%)
    psum x3, waiting for transfers between devices, per_device(): whole = lax.psum(partial_value, 'term')  301 us
    all_gather x3, waiting for transfers between devices, per_device(): full_vector = lax.all_gather(vector, 'term', axis=1, tiled=True)  151 us
    psum x3, blocking collectives, per_device(): lax.psum((jnp.sum(vector * sig), jnp.sum(vector * vector)), ('sector', 't...  121 us
    another operation x3, loops' own time, apply_tasks(): return lax.fori_loop(first, last, one, partial_value)  95.6 us
    dot_general x21, matrix products, one(): inner = jnp.dot(block, rights[slot], precision=highest)  71 us
    dot_general x21, matrix products, one(): product = jnp.dot(lefts[slot], inner, precision=highest)  64.4 us
    psum x1, blocking collectives, rescale(): total = lax.psum(jnp.sum(vector * vector), ('sector', 'term'))  39.4 us
  transfers between devices with their start and end apart: 6, of which 6 were waited for; matrix products, arithmetic and copies ran while one was open for 0% of the time, Pallas kernels for 0%

commit v1 on v0

v1 whole, which is shorter than its diff:
```python
import functools

import jax
import jax.numpy as jnp
from jax import lax
from jax.experimental import pallas as pl
from jax.experimental.pallas import tpu as pltpu
from jax.sharding import PartitionSpec as P

STEPS = 3
VMEM_LIMIT = 14 * 1024 * 1024
F32 = jnp.float32
BF16 = jnp.bfloat16


def split(value):
    high = value.astype(BF16)
    return high, (value - high.astype(F32)).astype(BF16)


def dot3(a_high, a_low, b_high, b_low):
    def dot(a, b):
        return jnp.dot(a, b, preferred_element_type=F32)

    return dot(a_high, b_high) + (dot(a_high, b_low) + dot(a_low, b_high))


def call(kernel, name, info, arrays, results, flops, scratch=()):
    held = pl.BlockSpec(memory_space=pltpu.VMEM)
    return pl.pallas_call(
        kernel,
        in_specs=[pl.BlockSpec(memory_space=pltpu.SMEM)] + [held] * len(arrays),
        out_specs=[held] * len(results),
        out_shape=[pltpu.VMEM(shape, dtype) for shape, dtype in results],
        scratch_shapes=list(scratch),
        compiler_params=pltpu.CompilerParams(vmem_limit_bytes=VMEM_LIMIT),
        cost_estimate=pl.CostEstimate(flops=flops, bytes_accessed=0, transcendentals=0),
        name=name,
    )(info, *arrays)


class Place:
    def __init__(self, slots):
        self.target, self.ring, self.side = slots, 2 * slots, 2 * slots + 1
        self.count, self.limits = 2 * slots + 2, 2 * slots + 3


def split_kernel(at, info, operator, high, low):
    k = pl.program_id(0)

    @pl.when(k < info[at.count])
    def _():
        high[k], low[k] = split(operator[0])


def split_operators(info, operators, name):
    slots, width, _ = operators.shape
    at = Place(slots)
    return pl.pallas_call(
        functools.partial(split_kernel, at),
        grid_spec=pltpu.PrefetchScalarGridSpec(
            num_scalar_prefetch=1,
            grid=(slots - 1,),
            in_specs=[
                pl.BlockSpec(
                    (1, width, width), lambda k, info: (jnp.minimum(k, info[at.count] - 1), 0, 0)
                )
            ],
            out_specs=[pl.BlockSpec(memory_space=pltpu.VMEM)] * 2,
        ),
        out_shape=[pltpu.VMEM((slots - 1, width, width), BF16)] * 2,
        compiler_params=pltpu.CompilerParams(vmem_limit_bytes=VMEM_LIMIT),
        cost_estimate=pl.CostEstimate(
            flops=0, bytes_accessed=slots * width * width * 4, transcendentals=0
        ),
        name=name,
    )(info, operators)


def split_blocks(blocks, high, low):
    share = blocks[0].shape[1]
    for place, block in enumerate(blocks):
        rows = pl.ds(place * share, share)
        high[:, rows, :], low[:, rows, :] = split(block[...])


def lanes(value):
    total = jnp.sum(value, axis=tuple(range(value.ndim - 1)))[None]
    width = total.shape[1]
    return sum(total[:, c : c + 128] for c in range(0, width, 128))


def inner_kernel(at, ring, info, *refs):
    blocks = refs[:ring]
    right_high, right_low, out_high, out_low, high, low = refs[ring:]
    split_blocks(blocks, high, low)

    def one(k, carry):
        source = info[k]
        out_high[k], out_low[k] = split(
            dot3(high[source], low[source], right_high[k], right_low[k])
        )
        return carry

    lax.fori_loop(0, info[at.count], one, 0)


def inner_rows(at, info, blocks, right):
    ring = len(blocks)
    live, width, _ = right[0].shape
    sectors, share, _ = blocks[0].shape
    rows = ring * share
    return call(
        functools.partial(inner_kernel, at, ring),
        "inner_rows",
        info,
        [*blocks, *right],
        [((live, rows, width), BF16)] * 2,
        live * rows * width * width * 6,
        [pltpu.VMEM((sectors, rows, width), BF16)] * 2,
    )


def first_row(at, info, ring, share, offset, side):
    around = lax.rem(info[at.ring] + offset, ring)
    return pl.multiple_of((around * 2 + side) * share, share)


def outer_rows(at, info, k, ring, side, left, full, outs):
    share = outs[0].shape[1]
    picks = [pl.ds(first_row(at, info, ring, share, r, side), share) for r in range(ring)]
    high, low = (
        jnp.concatenate([part[k, pick, :] for pick in picks], axis=0) for part in left
    )
    product = dot3(high, low, full[0][k], full[1][k])
    target = info[at.target + k]
    for r in range(ring):
        outs[r][target] += product[r * share : (r + 1) * share]


def overlap(blocks, outs):
    return sum(lanes(block[...] * out[...]) for block, out in zip(blocks, outs))


def middle_kernel(at, ring, info, *refs):
    blocks, refs = refs[:ring], refs[ring:]
    part_high, part_low, right_high, right_low, left_high, left_low = refs[:6]
    full_high, full_low, dots = refs[6:9]
    outs = refs[9 : 9 + ring]
    high, low = refs[9 + ring :]
    share = blocks[0].shape[1]
    side = info[at.side]
    split_blocks(blocks, high, low)
    for out in outs:
        out[...] = jnp.zeros_like(out)

    def one(k, carry):
        source = info[k]
        inner_high, inner_low = split(
            dot3(high[source], low[source], right_high[k], right_low[k])
        )
        for r in range(ring):
            own = pl.ds(first_row(at, info, ring, share, r, side), share)
            other = pl.ds(first_row(at, info, ring, share, r, 1 - side), share)
            rows = slice(r * share, (r + 1) * share)
            full_high[k, own, :] = part_high[k, rows, :]
            full_low[k, own, :] = part_low[k, rows, :]
            full_high[k, other, :] = inner_high[rows]
            full_low[k, other, :] = inner_low[rows]
        outer_rows(
            at, info, k, ring, 1 - side, (left_high, left_low), (full_high, full_low), outs
        )
        return carry

    lax.fori_loop(0, info[at.count], one, 0)
    dots[...] = overlap(blocks, outs)


def middle(at, info, blocks, part, right, left):
    ring = len(blocks)
    live, width, _ = right[0].shape
    sectors, share, _ = blocks[0].shape
    rows = ring * share
    results = call(
        functools.partial(middle_kernel, at, ring),
        "middle",
        info,
        [*blocks, *part, *right, *left],
        [((live, width, width), BF16)] * 2 + [((1, 128), F32)] + [(blocks[0].shape, F32)] * ring,
        live * rows * width * width * 12,
        [pltpu.VMEM((sectors, rows, width), BF16)] * 2,
    )
    return results[:2], results[2], results[3:]


def outer_kernel(at, ring, info, *refs):
    blocks, refs = refs[:ring], refs[ring:]
    full_high, full_low, left_high, left_low, dots_other, squares, sums = refs[:7]
    outs = refs[7:]
    for out in outs:
        out[...] = jnp.zeros_like(out)

    def one(k, carry):
        outer_rows(
            at, info, k, ring, info[at.side], (left_high, left_low), (full_high, full_low), outs
        )
        return carry

    lax.fori_loop(0, info[at.count], one, 0)
    row = lax.broadcasted_iota(jnp.int32, sums.shape, 0)
    dots = overlap(blocks, outs) + dots_other[...]
    sums[...] = jnp.where(row == 0, dots, jnp.where(row == 1, squares[...], 0.0))


def outer_own(at, info, blocks, full, left, dots_other, squares):
    ring = len(blocks)
    live, width, _ = left[0].shape
    share = blocks[0].shape[1]
    results = call(
        functools.partial(outer_kernel, at, ring),
        "outer_own",
        info,
        [*blocks, *full, *left, dots_other, squares],
        [((8, 128), F32)] + [(blocks[0].shape, F32)] * ring,
        live * ring * share * width * width * 6,
    )
    return results[0], results[1:]


def inside(at, info, shape, ring):
    share = shape[1]
    start = (info[at.ring] * 2 + info[at.side]) * share
    rows = start + lax.broadcasted_iota(jnp.int32, shape[1:], 0)
    cols = lax.broadcasted_iota(jnp.int32, shape[1:], 1)
    return [
        ((rows < info[at.limits + s]) & (cols < info[at.limits + s])).astype(F32)
        for s in range(shape[0])
    ]


def begin_kernel(at, ring, info, trial, vector, squares):
    total = jnp.zeros(squares.shape, F32)
    for s, mask in enumerate(inside(at, info, trial.shape, ring)):
        value = mask * trial[s]
        vector[s] = value
        total = total + lanes(value * value)
    squares[...] = total


def begin(at, info, trial, ring):
    return call(
        functools.partial(begin_kernel, at, ring),
        "begin",
        info,
        [trial],
        [(trial.shape, F32), ((1, 128), F32)],
        trial.size * 4,
    )


def update_kernel(at, ring, info, *refs):
    vector, precond, sums = refs[:3]
    terms, (result, squares, ritz) = refs[3:-3], refs[-3:]
    both = jnp.sum(sums[...], axis=1, keepdims=True)
    theta = both[0:1] / both[1:2]
    ritz[...] = jnp.broadcast_to(theta, ritz.shape)
    total = jnp.zeros(squares.shape, F32)
    for s, mask in enumerate(inside(at, info, vector.shape, ring)):
        sig = mask * sum(term[s] for term in terms)
        value = vector[s] - (sig - theta * vector[s]) / precond[s]
        result[s] = value
        total = total + lanes(value * value)
    squares[...] = total


def update(at, info, vector, precond, sums, terms, ring):
    return call(
        functools.partial(update_kernel, at, ring),
        "update",
        info,
        [vector, precond, sums, *terms],
        [(vector.shape, F32), ((1, 128), F32), ((1, 128), F32)],
        vector.size * 8,
    )


def across(value, terms):
    return lax.ppermute(value, "term", [(i, i ^ 1) for i in range(terms)])


def around(value, terms, shift):
    return lax.ppermute(value, "term", [(i, (i + 2 * shift) % terms) for i in range(terms)])


def gather_own(block, terms):
    ring = terms // 2
    blocks = {0: block}
    ups = ring // 2
    downs = ring - 1 - ups
    for hop in range(1, ups + 1):
        blocks[(ring - hop) % ring] = around(blocks[(ring - hop + 1) % ring], terms, 1)
        if hop <= downs:
            blocks[hop] = around(blocks[hop - 1], terms, -1)
    return [blocks[r] for r in range(ring)]


def total_sum(values, sectors, terms):
    for axis, size in (("sector", sectors), ("term", terms)):
        if size & (size - 1):
            values = lax.psum(values, axis)
            continue
        step = 1
        while step < size:
            values = values + lax.ppermute(values, axis, [(i, i ^ step) for i in range(size)])
            step *= 2
    return values


def scatter_sum(own, other, terms):
    ring = terms // 2
    ups = ring // 2
    downs = ring - 1 - ups
    order = []
    for hop in range(ups, 0, -1):
        order.append(hop)
        if hop <= downs:
            order.append((ring - hop) % ring)
    order.append(0)
    received = {r: across(other[r], terms) for r in order}
    up = down = None
    for hop in range(ups, 0, -1):
        value = own[hop] + received[hop]
        up = around(value if up is None else value + up, terms, 1)
        if hop <= downs:
            back = (ring - hop) % ring
            value = own[back] + received[back]
            down = around(value if down is None else value + down, terms, -1)
    return [term for term in (own[0], received[0], up, down) if term is not None]


def per_device(
    trial, precond, sector_dims, left_ops, right_ops, task_source, task_target, task_count
):
    sec_dev, share, width = trial.shape
    slots = left_ops.shape[0]
    sectors, terms = lax.axis_size("sector"), lax.axis_size("term")
    ring = terms // 2
    cells = float(sec_dev * sectors * width * width)
    term = lax.axis_index("term").astype(jnp.int32)
    at = Place(slots)
    info = jnp.concatenate(
        [task_source, task_target, jnp.stack([term // 2, term % 2]), task_count, sector_dims]
    )
    values = []
    vector, squares = begin(at, info, trial, ring)
    right = split_operators(info, right_ops, "split_right")
    left = split_operators(info, left_ops, "split_left")
    for step in range(STEPS):
        mine = gather_own(vector, terms)
        theirs = [across(block, terms) for block in mine]
        part = inner_rows(at, info, mine, right)
        full, dots_other, outs_other = middle(at, info, theirs, part, right, left)
        sums, outs_own = outer_own(at, info, mine, full, left, dots_other, squares)
        sums = total_sum(sums, sectors, terms)
        summed = scatter_sum(outs_own, outs_other, terms)
        vector, squares, ritz = update(at, info, vector, precond, sums, summed, ring)
        values.append(ritz[0, :1])
    total = jnp.sum(total_sum(squares, sectors, terms))
    return (vector * jnp.sqrt(cells / total), jnp.concatenate(values))


def solution(mesh):
    return jax.shard_map(
        per_device,
        mesh=mesh,
        in_specs=(
            P("sector", "term", None),
            P("sector", "term", None),
            P("sector"),
            P(("sector", "term"), None, None),
            P(("sector", "term"), None, None),
            P(("sector", "term")),
            P(("sector", "term")),
            P(("sector", "term")),
        ),
        out_specs=(P("sector", "term", None), P()),
        check_vma=False,
    )
```

time: 911 us -> 269 us (0.30)
  waiting for transfers between devices: 452 us -> 112 us
  blocking collectives: 161 us -> 0 us
  matrix products: 135 us -> 0 us
  loops' own time: 95.6 us -> 0 us
  starting transfers between devices: 0.25 us -> 84.2 us
  Pallas kernels: 0 us -> 61.8 us
  local copies, waits for them, and re-layouts: 29.5 us -> 6.76 us
  between operations: 19 us -> 2.38 us
  other arithmetic: 15 us -> 2.42 us
    psum x3 -> x0, waiting for transfers between devices: 301 us -> none  [per_device(): whole = lax.psum(partial_value, 'term')]
    psum x4 -> x0, blocking collectives: 161 us -> none  [the longest x3 121 us: per_device(): lax.psum((jnp.sum(vector * sig), jnp.sum(vector * vector)), ('sector', 't...]
    all_gather x3 -> x0, waiting for transfers between devices: 151 us -> none  [per_device(): full_vector = lax.all_gather(vector, 'term', axis=1, tiled=True)]
    dot_general x42 -> x0, matrix products: 135 us -> none  [the longest x21 71 us: one(): inner = jnp.dot(block, rights[slot], precision=highest)]
    ppermute x0 -> x62, waiting for transfers between devices: none -> 112 us  [the longest x20 42.6 us: total_sum(): lax.ppermute(values, axis, [(i, i ^ step) for i in range(size)])]
    another operation x3 -> x0, loops' own time: 95.6 us -> none  [apply_tasks(): return lax.fori_loop(first, last, one, partial_value)]
    ppermute x0 -> x62, starting transfers between devices: none -> 84.2 us  [the longest x20 35.5 us: total_sum(): lax.ppermute(values, axis, [(i, i ^ step) for i in range(size)])]
    pallas_call x0 -> x15, Pallas kernels: none -> 61.8 us  [the longest x13 58.4 us: call(): pl.pallas_call(kernel, in_specs=[pl.BlockSpec(memory_space=pltpu.SMEM)] +...]
  transfers between devices with their start and end apart: 6 -> 62, of which waited for: 6 -> 43; matrix products, arithmetic and copies ran while one was open for 0% -> 0% of each run, Pallas kernels for 0% -> 12%
where the time goes in v1:
time: 269 us; the launch traced here: 270 us
  waiting for transfers between devices  112 us (42%)
  starting transfers between devices  84.2 us (31%)
  Pallas kernels  61.8 us (23%)
  local copies, waits for them, and re-layouts  6.76 us (3%)
    pallas_call x13, Pallas kernels, call(): pl.pallas_call(kernel, in_specs=[pl.BlockSpec(memory_space=pltpu.SMEM)] +...  58.4 us
    ppermute x20, waiting for transfers between devices, total_sum(): lax.ppermute(values, axis, [(i, i ^ step) for i in range(size)])  42.6 us
    ppermute x18, waiting for transfers between devices, around(): lax.ppermute(value, 'term', [(i, (i + 2 * shift) % terms) for i in range(...  36 us
    ppermute x20, starting transfers between devices, total_sum(): lax.ppermute(values, axis, [(i, i ^ step) for i in range(size)])  35.5 us
    ppermute x24, waiting for transfers between devices, across(): return lax.ppermute(value, 'term', [(i, i ^ 1) for i in range(terms)])  33.6 us
    ppermute x18, starting transfers between devices, around(): lax.ppermute(value, 'term', [(i, (i + 2 * shift) % terms) for i in range(...  28.1 us
    ppermute x24, starting transfers between devices, across(): return lax.ppermute(value, 'term', [(i, i ^ 1) for i in range(terms)])  20.7 us
    unnamed x8, local copies, waits for them, and re-layouts  6 us
  transfers between devices with their start and end apart: 62, of which 43 were waited for; matrix products, arithmetic and copies ran while one was open for 0% of the time, Pallas kernels for 12%

profile of v1, /device:TPU:0, one launch (start us, length us, event | category | flops | bytes accessed | tf_op | source)
XLA Modules:
  0.0 269.8 jit_solution(17738522843760961621)
XLA Ops:
  8.8 7.1 %collective-permute-done.1.refs_3_ = f32[2,64,512]{2,1,0:T(8,128)S(1)} collective-permute-done((f32[2,64,512]{2,1,0:T(8,128)S(1)}, f32[2,64,512]{2,1,0:T(8,128)S(1)}, u32[]{:S(2)}, u32[]{:S(2)}) %collective-permute-start.1) | collective-permute-done | bytes 262176 | tf_op jit(solution)/shard_map/ppermute | solution.py:292
  28.3 4.7 %inner_rows.3 = (bf16[7,256,512]{2,1,0:T(8,128)(2,1)S(1)}, bf16[7,256,512]{2,1,0:T(8,128)(2,1)S(1)}) custom-call(s32[21]{0:T(128)S(1)} %concatenate.6.info, f32[2,64,512]{2,1,0:T(8,128)S(1)} %get-tuple-element.59.refs_0_, f32[2,64,512]{2,1,0:T(8,128)S(1)} %collective-permute-done.refs_1_, f32[2,64,512]{2,1,0:T(8,128)S(1)} %collective-permute-done.2.refs_2_, ...), custom_call_target="tpu_custom_call" | custom-call | flops 2818572288 | tf_op jit(solution)/shard_map/inner_rows/pallas_call | solution.py:30
  35.4 4.6 %collective-permute-done.4.refs_1_ = f32[2,64,512]{2,1,0:T(8,128)S(1)} collective-permute-done((f32[2,64,512]{2,1,0:T(8,128)S(1)}, f32[2,64,512]{2,1,0:T(8,128)S(1)}, u32[]{:S(2)}, u32[]{:S(2)}) %collective-permute-start.4) | collective-permute-done | bytes 262176 | tf_op jit(solution)/shard_map/ppermute | solution.py:288
  42.9 9.0 %middle.3 = (bf16[7,512,512]{2,1,0:T(8,128)(2,1)S(1)}, bf16[7,512,512]{2,1,0:T(8,128)(2,1)S(1)}, f32[1,128]{1,0:T(1,128)S(1)}, f32[2,64,512]{2,1,0:T(8,128)S(1)}...) custom-call(s32[21]{0:T(128)S(1)} %concatenate.6.info, ...), custom_call_target="tpu_custom_call" | custom-call | flops 5637144576 | tf_op jit(solution)/shard_map/middle/pallas_call | solution.py:30
  54.1 4.7 %outer_own.3 = (f32[8,128]{1,0:T(8,128)S(1)}, f32[2,64,512]{2,1,0:T(8,128)S(1)}, f32[2,64,512]{2,1,0:T(8,128)S(1)}, f32[2,64,512]{2,1,0:T(8,128)S(1)}, f32[2,64,512]{2,1,0:T(8,128)S(1)}) custom-call(s32[21]{0:T(128)S(1)} %concatenate.6.info, f32[2,64,512]{2,1,0:T(8,128)S(1)} %get-tuple-element.59.refs_0_, f32[2,64,512]{2,1,0:T(8,128)S(1)} %collective-permute-done.refs_1_, ...), custom_call_target="tpu_custom_call" | custom-call | flops 2818572288 | tf_op jit(solution)/shard_map/outer_own/pallas_call | solution.py:30
  58.8 5.4 %collective-permute-done.14 = f32[2,64,512]{2,1,0:T(8,128)S(1)} collective-permute-done((f32[2,64,512]{2,1,0:T(8,128)S(1)}, f32[2,64,512]{2,1,0:T(8,128)S(1)}, u32[]{:S(2)}, u32[]{:S(2)}) %collective-permute-start.14) | collective-permute-done | bytes 262176 | tf_op jit(solution)/shard_map/ppermute | solution.py:288
  67.1 5.1 %collective-permute-start.18 = (f32[2,64,512]{2,1,0:T(8,128)S(1)}, f32[2,64,512]{2,1,0:T(8,128)S(1)}, u32[]{:S(2)}, u32[]{:S(2)}) collective-permute-start(f32[2,64,512]{2,1,0:T(8,128)S(1)} %add.110), channel_id=1, source_target_pairs={{0,6},{1,7},{2,0},{3,1},{4,2},{5,3},{6,4},{7,5},{8,14},{9,15},{10,... | collective-permute-start | bytes 786440 | tf_op jit(solution)/shard_map/ppermute | solution.py:292
  76.2 5.3 %collective-permute-start.8 = (f32[8,128]{1,0:T(8,128)S(1)}, f32[8,128]{1,0:T(8,128)S(1)}, u32[]{:S(2)}, u32[]{:S(2)}) collective-permute-start(f32[8,128]{1,0:T(8,128)S(1)} %add.102), channel_id=1, source_target_pairs={{0,16},{8,24},{16,0},{24,8},{1,17},{9,25},{17,1},{25,9},{2,18},{10... | collective-permute-start | bytes 12296 | tf_op jit(solution)/shard_map/ppermute | solution.py:314
  83.1 3.6 %collective-permute-done.9 = f32[8,128]{1,0:T(8,128)S(1)} collective-permute-done((f32[8,128]{1,0:T(8,128)S(1)}, f32[8,128]{1,0:T(8,128)S(1)}, u32[]{:S(2)}, u32[]{:S(2)}) %collective-permute-start.9) | collective-permute-done | bytes 4128 | tf_op jit(solution)/shard_map/ppermute | solution.py:314
  99.9 6.6 %collective-permute-done.20.refs_3_ = f32[2,64,512]{2,1,0:T(8,128)S(1)} collective-permute-done((f32[2,64,512]{2,1,0:T(8,128)S(1)}, f32[2,64,512]{2,1,0:T(8,128)S(1)}, u32[]{:S(2)}, u32[]{:S(2)}) %collective-permute-start.20) | collective-permute-done | bytes 262176 | tf_op jit(solution)/shard_map/ppermute | solution.py:292
  110.6 4.1 %collective-permute-done.21.refs_2_ = f32[2,64,512]{2,1,0:T(8,128)S(1)} collective-permute-done((f32[2,64,512]{2,1,0:T(8,128)S(1)}, f32[2,64,512]{2,1,0:T(8,128)S(1)}, u32[]{:S(2)}, u32[]{:S(2)}) %collective-permute-start.21) | collective-permute-done | bytes 262176 | tf_op jit(solution)/shard_map/ppermute | solution.py:292
  114.9 4.8 %inner_rows.4 = (bf16[7,256,512]{2,1,0:T(8,128)(2,1)S(1)}, bf16[7,256,512]{2,1,0:T(8,128)(2,1)S(1)}) custom-call(s32[21]{0:T(128)S(1)} %concatenate.6.info, f32[2,64,512]{2,1,0:T(8,128)S(1)} %get-tuple-element.79.refs_0_, f32[2,64,512]{2,1,0:T(8,128)S(1)} %collective-permute-done.19.refs_1_, f32[2,64,512]{2,1,0:T(8,128)S(1)} %collective-permute-done.21.refs_2_, ...), custom_call_target="tpu_custom_call" | custom-call | flops 2818572288 | tf_op jit(solution)/shard_map/inner_rows/pallas_call | solution.py:30
  125.1 9.0 %middle.4 = (bf16[7,512,512]{2,1,0:T(8,128)(2,1)S(1)}, bf16[7,512,512]{2,1,0:T(8,128)(2,1)S(1)}, f32[1,128]{1,0:T(1,128)S(1)}, f32[2,64,512]{2,1,0:T(8,128)S(1)}...) custom-call(s32[21]{0:T(128)S(1)} %concatenate.6.info, ...), custom_call_target="tpu_custom_call" | custom-call | flops 5637144576 | tf_op jit(solution)/shard_map/middle/pallas_call | solution.py:30
  136.3 4.7 %outer_own.4 = (f32[8,128]{1,0:T(8,128)S(1)}, f32[2,64,512]{2,1,0:T(8,128)S(1)}, f32[2,64,512]{2,1,0:T(8,128)S(1)}, f32[2,64,512]{2,1,0:T(8,128)S(1)}, f32[2,64,512]{2,1,0:T(8,128)S(1)}) custom-call(s32[21]{0:T(128)S(1)} %concatenate.6.info, f32[2,64,512]{2,1,0:T(8,128)S(1)} %get-tuple-element.79.refs_0_, f32[2,64,512]{2,1,0:T(8,128)S(1)} %collective-permute-done.19.refs_1_, ...), custom_call_target="tpu_custom_call" | custom-call | flops 2818572288 | tf_op jit(solution)/shard_map/outer_own/pallas_call | solution.py:30
  146.2 3.8 %collective-permute-start.37 = (f32[2,64,512]{2,1,0:T(8,128)S(1)}, f32[2,64,512]{2,1,0:T(8,128)S(1)}, u32[]{:S(2)}, u32[]{:S(2)}) collective-permute-start(f32[2,64,512]{2,1,0:T(8,128)S(1)} %add.119), channel_id=1, source_target_pairs={{0,6},{1,7},{2,0},{3,1},{4,2},{5,3},{6,4},{7,5},{8,14},{9,15},{10,... | collective-permute-start | bytes 786440 | tf_op jit(solution)/shard_map/ppermute | solution.py:292
  153.1 6.1 %collective-permute-start.27 = (f32[8,128]{1,0:T(8,128)S(1)}, f32[8,128]{1,0:T(8,128)S(1)}, u32[]{:S(2)}, u32[]{:S(2)}) collective-permute-start(f32[8,128]{1,0:T(8,128)S(1)} %add.111), channel_id=1, source_target_pairs={{0,16},{8,24},{16,0},{24,8},{1,17},{9,25},{17,1},{25,9},{2,18},{10... | collective-permute-start | bytes 12296 | tf_op jit(solution)/shard_map/ppermute | solution.py:314
  160.8 3.6 %collective-permute-done.28 = f32[8,128]{1,0:T(8,128)S(1)} collective-permute-done((f32[8,128]{1,0:T(8,128)S(1)}, f32[8,128]{1,0:T(8,128)S(1)}, u32[]{:S(2)}, u32[]{:S(2)}) %collective-permute-start.28) | collective-permute-done | bytes 4128 | tf_op jit(solution)/shard_map/ppermute | solution.py:314
  177.6 6.6 %collective-permute-done.39.refs_3_ = f32[2,64,512]{2,1,0:T(8,128)S(1)} collective-permute-done((f32[2,64,512]{2,1,0:T(8,128)S(1)}, f32[2,64,512]{2,1,0:T(8,128)S(1)}, u32[]{:S(2)}, u32[]{:S(2)}) %collective-permute-start.39) | collective-permute-done | bytes 262176 | tf_op jit(solution)/shard_map/ppermute | solution.py:292
  188.3 4.1 %collective-permute-done.40.refs_2_ = f32[2,64,512]{2,1,0:T(8,128)S(1)} collective-permute-done((f32[2,64,512]{2,1,0:T(8,128)S(1)}, f32[2,64,512]{2,1,0:T(8,128)S(1)}, u32[]{:S(2)}, u32[]{:S(2)}) %collective-permute-start.40) | collective-permute-done | bytes 262176 | tf_op jit(solution)/shard_map/ppermute | solution.py:292
  192.6 4.8 %inner_rows.5 = (bf16[7,256,512]{2,1,0:T(8,128)(2,1)S(1)}, bf16[7,256,512]{2,1,0:T(8,128)(2,1)S(1)}) custom-call(s32[21]{0:T(128)S(1)} %concatenate.6.info, f32[2,64,512]{2,1,0:T(8,128)S(1)} %get-tuple-element.95.refs_0_, f32[2,64,512]{2,1,0:T(8,128)S(1)} %collective-permute-done.38.refs_1_, f32[2,64,512]{2,1,0:T(8,128)S(1)} %collective-permute-done.40.refs_2_, ...), custom_call_target="tpu_custom_call" | custom-call | flops 2818572288 | tf_op jit(solution)/shard_map/inner_rows/pallas_call | solution.py:30
  202.8 9.0 %middle.5 = (bf16[7,512,512]{2,1,0:T(8,128)(2,1)S(1)}, bf16[7,512,512]{2,1,0:T(8,128)(2,1)S(1)}, f32[1,128]{1,0:T(1,128)S(1)}, f32[2,64,512]{2,1,0:T(8,128)S(1)}...) custom-call(s32[21]{0:T(128)S(1)} %concatenate.6.info, ...), custom_call_target="tpu_custom_call" | custom-call | flops 5637144576 | tf_op jit(solution)/shard_map/middle/pallas_call | solution.py:30
  214.0 4.7 %outer_own.5 = (f32[8,128]{1,0:T(8,128)S(1)}, f32[2,64,512]{2,1,0:T(8,128)S(1)}, f32[2,64,512]{2,1,0:T(8,128)S(1)}, f32[2,64,512]{2,1,0:T(8,128)S(1)}, f32[2,64,512]{2,1,0:T(8,128)S(1)}) custom-call(s32[21]{0:T(128)S(1)} %concatenate.6.info, f32[2,64,512]{2,1,0:T(8,128)S(1)} %get-tuple-element.95.refs_0_, f32[2,64,512]{2,1,0:T(8,128)S(1)} %collective-permute-done.38.refs_1_, ...), custom_call_target="tpu_custom_call" | custom-call | flops 2818572288 | tf_op jit(solution)/shard_map/outer_own/pallas_call | solution.py:30
  223.9 3.8 %collective-permute-start.56 = (f32[2,64,512]{2,1,0:T(8,128)S(1)}, f32[2,64,512]{2,1,0:T(8,128)S(1)}, u32[]{:S(2)}, u32[]{:S(2)}) collective-permute-start(f32[2,64,512]{2,1,0:T(8,128)S(1)} %add.128), channel_id=1, source_target_pairs={{0,6},{1,7},{2,0},{3,1},{4,2},{5,3},{6,4},{7,5},{8,14},{9,15},{10,... | collective-permute-start | bytes 786440 | tf_op jit(solution)/shard_map/ppermute | solution.py:292
  230.8 6.2 %collective-permute-start.46 = (f32[8,128]{1,0:T(8,128)S(1)}, f32[8,128]{1,0:T(8,128)S(1)}, u32[]{:S(2)}, u32[]{:S(2)}) collective-permute-start(f32[8,128]{1,0:T(8,128)S(1)} %add.120), channel_id=1, source_target_pairs={{0,16},{8,24},{16,0},{24,8},{1,17},{9,25},{17,1},{25,9},{2,18},{10... | collective-permute-start | bytes 12296 | tf_op jit(solution)/shard_map/ppermute | solution.py:314
  (155 shorter events, 135.9 us)
Async XLA Ops:
  3.6 12.3 %collective-permute-start.1 = (f32[2,64,512]{2,1,0:T(8,128)S(1)}, f32[2,64,512]{2,1,0:T(8,128)S(1)}, u32[]{:S(2)}, u32[]{:S(2)}) collective-permute-start(f32[2,64,512]{2,1,0:T(8,128)S(1)} %get-tuple-element.59.refs_0_), channel_id=1, source_target_pairs={{0,2},{1,3},{2,4},{3,5},{4,6},{5,7},{6,0},{7,1},{8,10},{9,11},{10,... | collective-permute-start | bytes 786440 | tf_op jit(solution)/shard_map/ppermute | solution.py:292
  6.7 19.5 %collective-permute-start = (f32[2,64,512]{2,1,0:T(8,128)S(1)}, f32[2,64,512]{2,1,0:T(8,128)S(1)}, u32[]{:S(2)}, u32[]{:S(2)}) collective-permute-start(f32[2,64,512]{2,1,0:T(8,128)S(1)} %get-tuple-element.59.refs_0_), channel_id=1, source_target_pairs={{0,6},{1,7},{2,0},{3,1},{4,2},{5,3},{6,4},{7,5},{8,14},{9,15},{10,... | collective-permute-start | bytes 786440 | tf_op jit(solution)/shard_map/ppermute | solution.py:292
  15.9 12.3 %collective-permute-start.2 = (f32[2,64,512]{2,1,0:T(8,128)S(1)}, f32[2,64,512]{2,1,0:T(8,128)S(1)}, u32[]{:S(2)}, u32[]{:S(2)}) collective-permute-start(f32[2,64,512]{2,1,0:T(8,128)S(1)} %collective-permute-done.1.refs_3_), channel_id=1, source_target_pairs={{0,2},{1,3},{2,4},{3,5},{4,6},{5,7},{6,0},{7,1},{8,10},{9,11},{10,... | collective-permute-start | bytes 786440 | tf_op jit(solution)/shard_map/ppermute | solution.py:292
  15.9 17.2 %collective-permute-start.3 = (f32[2,64,512]{2,1,0:T(8,128)S(1)}, f32[2,64,512]{2,1,0:T(8,128)S(1)}, u32[]{:S(2)}, u32[]{:S(2)}) collective-permute-start(f32[2,64,512]{2,1,0:T(8,128)S(1)} %get-tuple-element.59.refs_0_), channel_id=1, source_target_pairs={{0,1},{1,0},{2,3},{3,2},{4,5},{5,4},{6,7},{7,6},{8,9},{9,8},{10,11... | collective-permute-start | bytes 786440 | tf_op jit(solution)/shard_map/ppermute | solution.py:288
  26.2 13.8 %collective-permute-start.4 = (f32[2,64,512]{2,1,0:T(8,128)S(1)}, f32[2,64,512]{2,1,0:T(8,128)S(1)}, u32[]{:S(2)}, u32[]{:S(2)}) collective-permute-start(f32[2,64,512]{2,1,0:T(8,128)S(1)} %collective-permute-done.refs_1_), channel_id=1, source_target_pairs={{0,1},{1,0},{2,3},{3,2},{4,5},{5,4},{6,7},{7,6},{8,9},{9,8},{10,11... | collective-permute-start | bytes 786440 | tf_op jit(solution)/shard_map/ppermute | solution.py:288
  28.2 14.6 %collective-permute-start.5 = (f32[2,64,512]{2,1,0:T(8,128)S(1)}, f32[2,64,512]{2,1,0:T(8,128)S(1)}, u32[]{:S(2)}, u32[]{:S(2)}) collective-permute-start(f32[2,64,512]{2,1,0:T(8,128)S(1)} %collective-permute-done.2.refs_2_), channel_id=1, source_target_pairs={{0,1},{1,0},{2,3},{3,2},{4,5},{5,4},{6,7},{7,6},{8,9},{9,8},{10,11... | collective-permute-start | bytes 786440 | tf_op jit(solution)/shard_map/ppermute | solution.py:288
  51.9 20.3 %collective-permute-start.13 = (f32[2,64,512]{2,1,0:T(8,128)S(1)}, f32[2,64,512]{2,1,0:T(8,128)S(1)}, u32[]{:S(2)}, u32[]{:S(2)}) collective-permute-start(f32[2,64,512]{2,1,0:T(8,128)S(1)} %get-tuple-element.74), channel_id=1, source_target_pairs={{0,1},{1,0},{2,3},{3,2},{4,5},{5,4},{6,7},{7,6},{8,9},{9,8},{10,11... | collective-permute-start | bytes 786440 | tf_op jit(solution)/shard_map/ppermute | solution.py:288
  52.0 12.3 %collective-permute-start.14 = (f32[2,64,512]{2,1,0:T(8,128)S(1)}, f32[2,64,512]{2,1,0:T(8,128)S(1)}, u32[]{:S(2)}, u32[]{:S(2)}) collective-permute-start(f32[2,64,512]{2,1,0:T(8,128)S(1)} %get-tuple-element.76), channel_id=1, source_target_pairs={{0,1},{1,0},{2,3},{3,2},{4,5},{5,4},{6,7},{7,6},{8,9},{9,8},{10,11... | collective-permute-start | bytes 786440 | tf_op jit(solution)/shard_map/ppermute | solution.py:288
  54.0 13.1 %collective-permute-start.17 = (f32[2,64,512]{2,1,0:T(8,128)S(1)}, f32[2,64,512]{2,1,0:T(8,128)S(1)}, u32[]{:S(2)}, u32[]{:S(2)}) collective-permute-start(f32[2,64,512]{2,1,0:T(8,128)S(1)} %get-tuple-element.78), channel_id=1, source_target_pairs={{0,1},{1,0},{2,3},{3,2},{4,5},{5,4},{6,7},{7,6},{8,9},{9,8},{10,11... | collective-permute-start | bytes 786440 | tf_op jit(solution)/shard_map/ppermute | solution.py:288
  64.4 30.9 %collective-permute-start.12 = (f32[2,64,512]{2,1,0:T(8,128)S(1)}, f32[2,64,512]{2,1,0:T(8,128)S(1)}, u32[]{:S(2)}, u32[]{:S(2)}) collective-permute-start(f32[2,64,512]{2,1,0:T(8,128)S(1)} %get-tuple-element.72), channel_id=1, source_target_pairs={{0,1},{1,0},{2,3},{3,2},{4,5},{5,4},{6,7},{7,6},{8,9},{9,8},{10,11... | collective-permute-start | bytes 786440 | tf_op jit(solution)/shard_map/ppermute | solution.py:288
  67.1 28.1 %collective-permute-start.18 = (f32[2,64,512]{2,1,0:T(8,128)S(1)}, f32[2,64,512]{2,1,0:T(8,128)S(1)}, u32[]{:S(2)}, u32[]{:S(2)}) collective-permute-start(f32[2,64,512]{2,1,0:T(8,128)S(1)} %add.110), channel_id=1, source_target_pairs={{0,6},{1,7},{2,0},{3,1},{4,2},{5,3},{6,4},{7,5},{8,14},{9,15},{10,... | collective-permute-start | bytes 786440 | tf_op jit(solution)/shard_map/ppermute | solution.py:292
  74.9 20.4 %collective-permute-start.16 = (f32[2,64,512]{2,1,0:T(8,128)S(1)}, f32[2,64,512]{2,1,0:T(8,128)S(1)}, u32[]{:S(2)}, u32[]{:S(2)}) collective-permute-start(f32[2,64,512]{2,1,0:T(8,128)S(1)} %add_add_fusion.2), channel_id=1, source_target_pairs={{0,2},{1,3},{2,4},{3,5},{4,6},{5,7},{6,0},{7,1},{8,10},{9,11},{10,... | collective-permute-start | bytes 786440 | tf_op jit(solution)/shard_map/ppermute | solution.py:292
  107.5 12.1 %collective-permute-start.22 = (f32[2,64,512]{2,1,0:T(8,128)S(1)}, f32[2,64,512]{2,1,0:T(8,128)S(1)}, u32[]{:S(2)}, u32[]{:S(2)}) collective-permute-start(f32[2,64,512]{2,1,0:T(8,128)S(1)} %get-tuple-element.79.refs_0_), channel_id=1, source_target_pairs={{0,1},{1,0},{2,3},{3,2},{4,5},{5,4},{6,7},{7,6},{8,9},{9,8},{10,11... | collective-permute-start | bytes 786440 | tf_op jit(solution)/shard_map/ppermute | solution.py:288
  107.5 12.1 %collective-permute-start.25 = (f32[2,64,512]{2,1,0:T(8,128)S(1)}, f32[2,64,512]{2,1,0:T(8,128)S(1)}, u32[]{:S(2)}, u32[]{:S(2)}) collective-permute-start(f32[2,64,512]{2,1,0:T(8,128)S(1)} %collective-permute-done.20.refs_3_), channel_id=1, source_target_pairs={{0,1},{1,0},{2,3},{3,2},{4,5},{5,4},{6,7},{7,6},{8,9},{9,8},{10,11... | collective-permute-start | bytes 786440 | tf_op jit(solution)/shard_map/ppermute | solution.py:288
  134.1 15.9 %collective-permute-start.32 = (f32[2,64,512]{2,1,0:T(8,128)S(1)}, f32[2,64,512]{2,1,0:T(8,128)S(1)}, u32[]{:S(2)}, u32[]{:S(2)}) collective-permute-start(f32[2,64,512]{2,1,0:T(8,128)S(1)} %get-tuple-element.90), channel_id=1, source_target_pairs={{0,1},{1,0},{2,3},{3,2},{4,5},{5,4},{6,7},{7,6},{8,9},{9,8},{10,11... | collective-permute-start | bytes 786440 | tf_op jit(solution)/shard_map/ppermute | solution.py:288
  143.5 29.4 %collective-permute-start.31 = (f32[2,64,512]{2,1,0:T(8,128)S(1)}, f32[2,64,512]{2,1,0:T(8,128)S(1)}, u32[]{:S(2)}, u32[]{:S(2)}) collective-permute-start(f32[2,64,512]{2,1,0:T(8,128)S(1)} %get-tuple-element.88), channel_id=1, source_target_pairs={{0,1},{1,0},{2,3},{3,2},{4,5},{5,4},{6,7},{7,6},{8,9},{9,8},{10,11... | collective-permute-start | bytes 786440 | tf_op jit(solution)/shard_map/ppermute | solution.py:288
  146.2 26.7 %collective-permute-start.37 = (f32[2,64,512]{2,1,0:T(8,128)S(1)}, f32[2,64,512]{2,1,0:T(8,128)S(1)}, u32[]{:S(2)}, u32[]{:S(2)}) collective-permute-start(f32[2,64,512]{2,1,0:T(8,128)S(1)} %add.119), channel_id=1, source_target_pairs={{0,6},{1,7},{2,0},{3,1},{4,2},{5,3},{6,4},{7,5},{8,14},{9,15},{10,... | collective-permute-start | bytes 786440 | tf_op jit(solution)/shard_map/ppermute | solution.py:292
  151.8 21.2 %collective-permute-start.35 = (f32[2,64,512]{2,1,0:T(8,128)S(1)}, f32[2,64,512]{2,1,0:T(8,128)S(1)}, u32[]{:S(2)}, u32[]{:S(2)}) collective-permute-start(f32[2,64,512]{2,1,0:T(8,128)S(1)} %add_add_fusion.1), channel_id=1, source_target_pairs={{0,2},{1,3},{2,4},{3,5},{4,6},{5,7},{6,0},{7,1},{8,10},{9,11},{10,... | collective-permute-start | bytes 786440 | tf_op jit(solution)/shard_map/ppermute | solution.py:292
  185.2 12.1 %collective-permute-start.41 = (f32[2,64,512]{2,1,0:T(8,128)S(1)}, f32[2,64,512]{2,1,0:T(8,128)S(1)}, u32[]{:S(2)}, u32[]{:S(2)}) collective-permute-start(f32[2,64,512]{2,1,0:T(8,128)S(1)} %get-tuple-element.95.refs_0_), channel_id=1, source_target_pairs={{0,1},{1,0},{2,3},{3,2},{4,5},{5,4},{6,7},{7,6},{8,9},{9,8},{10,11... | collective-permute-start | bytes 786440 | tf_op jit(solution)/shard_map/ppermute | solution.py:288
  185.2 12.1 %collective-permute-start.44 = (f32[2,64,512]{2,1,0:T(8,128)S(1)}, f32[2,64,512]{2,1,0:T(8,128)S(1)}, u32[]{:S(2)}, u32[]{:S(2)}) collective-permute-start(f32[2,64,512]{2,1,0:T(8,128)S(1)} %collective-permute-done.39.refs_3_), channel_id=1, source_target_pairs={{0,1},{1,0},{2,3},{3,2},{4,5},{5,4},{6,7},{7,6},{8,9},{9,8},{10,11... | collective-permute-start | bytes 786440 | tf_op jit(solution)/shard_map/ppermute | solution.py:288
  211.8 15.9 %collective-permute-start.51 = (f32[2,64,512]{2,1,0:T(8,128)S(1)}, f32[2,64,512]{2,1,0:T(8,128)S(1)}, u32[]{:S(2)}, u32[]{:S(2)}) collective-permute-start(f32[2,64,512]{2,1,0:T(8,128)S(1)} %get-tuple-element.106), channel_id=1, source_target_pairs={{0,1},{1,0},{2,3},{3,2},{4,5},{5,4},{6,7},{7,6},{8,9},{9,8},{10,11... | collective-permute-start | bytes 786440 | tf_op jit(solution)/shard_map/ppermute | solution.py:288
  221.2 29.5 %collective-permute-start.50 = (f32[2,64,512]{2,1,0:T(8,128)S(1)}, f32[2,64,512]{2,1,0:T(8,128)S(1)}, u32[]{:S(2)}, u32[]{:S(2)}) collective-permute-start(f32[2,64,512]{2,1,0:T(8,128)S(1)} %get-tuple-element.104), channel_id=1, source_target_pairs={{0,1},{1,0},{2,3},{3,2},{4,5},{5,4},{6,7},{7,6},{8,9},{9,8},{10,11... | collective-permute-start | bytes 786440 | tf_op jit(solution)/shard_map/ppermute | solution.py:288
  223.9 26.8 %collective-permute-start.56 = (f32[2,64,512]{2,1,0:T(8,128)S(1)}, f32[2,64,512]{2,1,0:T(8,128)S(1)}, u32[]{:S(2)}, u32[]{:S(2)}) collective-permute-start(f32[2,64,512]{2,1,0:T(8,128)S(1)} %add.128), channel_id=1, source_target_pairs={{0,6},{1,7},{2,0},{3,1},{4,2},{5,3},{6,4},{7,5},{8,14},{9,15},{10,... | collective-permute-start | bytes 786440 | tf_op jit(solution)/shard_map/ppermute | solution.py:292
  229.5 21.2 %collective-permute-start.54 = (f32[2,64,512]{2,1,0:T(8,128)S(1)}, f32[2,64,512]{2,1,0:T(8,128)S(1)}, u32[]{:S(2)}, u32[]{:S(2)}) collective-permute-start(f32[2,64,512]{2,1,0:T(8,128)S(1)} %add_add_fusion), channel_id=1, source_target_pairs={{0,2},{1,3},{2,4},{3,5},{4,6},{5,7},{6,0},{7,1},{8,10},{9,11},{10,... | collective-permute-start | bytes 786440 | tf_op jit(solution)/shard_map/ppermute | solution.py:292
  (42 other events, 308.6 us)
